TPU v7x, 32 devices: a whole 2x2x4 slice. The times are simulated.
32 devices in a mesh: dp: 8 (over y, x, core), vocab: 4 (over z).
Axes of the slice: x: 2, y: 2, z: 4, core: 2. Of those that a mesh axis runs over, the one named last changes fastest.
Arguments:
- student_hidden: bfloat16 [192, 3584], P('dp'), may hold values from -110 to 110
- teacher_hidden: bfloat16 [192, 4608], P('dp'), may hold values from -110 to 110
- student_head: bfloat16 [3584, 16384], P(None, ('dp', 'vocab')), may hold values from -0.09375 to 0.09375
- teacher_head: bfloat16 [4608, 16384], P(None, ('dp', 'vocab')), may hold values from -0.09375 to 0.09375
- live_count: int32 [8], P('dp'), may hold values from 1 to 24, as said below
- teacher_count: int32 [8], P('dp'), may hold values from 1 to 24, as said below
- teacher_dest: int32 [192], P('dp'), may hold values from 0 to 191, as said below
Outputs:
- distill_loss: float32 [], replicated
- grad_hidden: bfloat16 [192, 3584], P('dp', 'vocab')
- grad_head: bfloat16 [3584, 16384], P(None, ('dp', 'vocab'))
Inputs may be any that keep to these rules, and one draw needn't show every extreme that they name: Shard s's covered tokens are its first live_count[s] tokens; the counts sum to 96. Data shard j's filled teacher row slots are its first teacher_count[j] slots; the counts sum to 96. `teacher_dest`: A filled slot names the global index of a covered token; every covered token is named by exactly one filled slot. Unfilled slots hold arbitrary indices.
All inputs are finite; a program needn't handle non-finite values.
Results may differ from a plain program's by a relative error of at most 0.014.
Values may be sent and summed in bfloat16 or wider, within the bound.
A program may use at most 128 MiB of HBM per device.

v0:
```python
import jax
import jax.numpy as jnp
from jax import lax
from jax.sharding import PartitionSpec as P

loss_scale = 65536.0


def per_device(
    student_hidden,
    teacher_hidden,
    student_head,
    teacher_head,
    live_count,
    teacher_count,
    teacher_dest,
):
    tok_dev = student_hidden.shape[0]
    data_size = lax.axis_size("dp")
    token_count = tok_dev * data_size
    live_total = token_count // 2
    grad_scale = loss_scale / live_total
    live_all, teach_all, dest_all = (
        lax.all_gather(live_count, "dp", axis=0, tiled=True),
        lax.all_gather(teacher_count, "dp", axis=0, tiled=True),
        lax.all_gather(teacher_dest, "dp", axis=0, tiled=True),
    )
    position = lax.broadcasted_iota(jnp.int32, (data_size, tok_dev), 1)
    live_flag = (position < live_all[:, None]).reshape(-1)
    slot_ok = (position < teach_all[:, None]).reshape(-1)
    gathered = lax.all_gather(student_hidden, "dp", axis=0, tiled=True)
    vocab_rows = student_head.shape[1]
    student_logits = jnp.dot(gathered, student_head, preferred_element_type=jnp.float32)
    packed = jnp.dot(
        lax.all_gather(teacher_hidden, "dp", axis=0, tiled=True),
        teacher_head,
        preferred_element_type=jnp.float32,
    )
    target = jnp.where(slot_ok, dest_all, token_count)
    teacher_logits = (
        jnp.zeros((token_count, vocab_rows), jnp.float32).at[target].set(packed, mode="drop")
    )
    teacher_top, student_top = lax.pmax(
        (jnp.max(teacher_logits, axis=1), jnp.max(student_logits, axis=1)), ("dp", "vocab")
    )
    teacher_weights = jnp.exp(teacher_logits - teacher_top[:, None])
    teacher_sum, student_sum, cross_sum = lax.psum(
        (
            jnp.sum(teacher_weights, axis=1),
            jnp.sum(jnp.exp(student_logits - student_top[:, None]), axis=1),
            jnp.sum(teacher_weights * (teacher_logits - student_logits), axis=1),
        ),
        ("dp", "vocab"),
    )
    teacher_norm = teacher_top + jnp.log(teacher_sum)
    student_norm = student_top + jnp.log(student_sum)
    divergence = cross_sum / teacher_sum - teacher_norm + student_norm
    distill_loss = jnp.sum(jnp.where(live_flag, divergence, 0.0)) / live_total
    probs_gap = jnp.exp(student_logits - student_norm[:, None]) - jnp.exp(
        teacher_logits - teacher_norm[:, None]
    )
    logit_grad = jnp.where(live_flag[:, None], probs_gap * grad_scale, 0.0).astype(jnp.bfloat16)
    grad_head = lax.dot_general(
        gathered, logit_grad, (((0,), (0,)), ((), ())), preferred_element_type=jnp.float32
    ).astype(jnp.bfloat16)
    columns = student_head.shape[0] // lax.axis_size("vocab")
    summed = lax.psum(
        lax.dot_general(
            logit_grad, student_head, (((1,), (1,)), ((), ())), preferred_element_type=jnp.float32
        ),
        ("dp", "vocab"),
    )
    own_block = lax.dynamic_slice(
        summed,
        (lax.axis_index("dp") * tok_dev, lax.axis_index("vocab") * columns),
        (tok_dev, columns),
    )
    return (distill_loss, own_block.astype(jnp.bfloat16), grad_head)


def solution(mesh):
    return jax.shard_map(
        per_device,
        mesh=mesh,
        in_specs=(
            P("dp", None),
            P("dp", None),
            P(None, ("dp", "vocab")),
            P(None, ("dp", "vocab")),
            P("dp"),
            P("dp"),
            P("dp"),
        ),
        out_specs=(P(), P("dp", "vocab"), P(None, ("dp", "vocab"))),
        check_vma=False,
    )
```

profile of v0, /device:TPU:0, one launch (start us, length us, event | category | flops | bytes accessed | tf_op | source)
XLA Modules:
  0.0 252.2 jit_solution(3580026897521757931)
XLA Ops:
  7.2 0.0 all-gather.5.cloned.1.call-start
  7.2 0.7 all-gather.5.cloned.1.call-update
  7.9 0.0 all-gather.3.cloned.1.call-start
  7.9 0.7 all-gather.3.cloned.1.call-update
  9.9 1.2 dynamic-slice
  11.8 0.8 dynamic-update-slice
  12.6 0.8 dynamic-update-slice.1
  13.4 0.8 dynamic-update-slice.2
  14.2 9.5 %all-reduce.3 = (s32[8]{0:T(128)S(1)}, s32[8]{0:T(128)S(1)}, s32[192]{0:T(256)S(1)}) all-reduce(s32[8]{0:T(128)S(1)} %dynamic-update-slice, s32[8]{0:T(128)S(1)} %dynamic-update-slice.1, s32[192]{0:T(256)S(1)} %dynamic-update-slice.2), channel_id=1, replica_groups=mesh['dp'=8,'vocab'=4] {'dp'}, use_global_device_ids=true, to_apply=%add | all-reduce | flops 208 | bytes 1664
  23.7 0.1 iota_compare_fusion.1
  23.7 0.1 lt.42
  23.8 0.1 iota_compare_fusion
  23.9 0.1 lt.45
  24.0 13.6 %all-gather.5.cloned.1.call-done = bf16[192,3584]{1,0:T(8,128)(2,1)} async-done(((bf16[24,3584]{1,0:T(8,128)(2,1)}), bf16[192,3584]{1,0:T(8,128)(2,1)}) %all-gather.5.cloned.1.call-update) | async-done | bytes 1376272 | tf_op jit(solution)/shard_map/all_gather | solution.py:31
  37.6 3.4 %fusion.4 = (f32[192]{0:T(256)S(1)}, f32[192,512]{1,0:T(8,128)S(1)}) fusion(bf16[192,3584]{1,0:T(8,128)(2,1)} %all-gather.5.cloned.1.call-done, bf16[3584,512]{1,0:T(8,128)(2,1)} %param.9), kind=kOutput, calls=%fused_computation.17 | convolution fusion | flops 704741184 | bytes 5440256 | tf_op jit(solution)/shard_map/dot_general | solution.py:33
  41.0 25.0 %all-gather.3.cloned.1.call-done = bf16[192,4608]{1,0:T(8,128)(2,1)} async-done(((bf16[24,4608]{1,0:T(8,128)(2,1)}), bf16[192,4608]{1,0:T(8,128)(2,1)}) %all-gather.3.cloned.1.call-update) | async-done | bytes 1769488 | tf_op jit(solution)/shard_map/all_gather | solution.py:35
  66.0 4.0 %fusion.5 = f32[192,512]{1,0:T(8,128)S(1)} fusion(bf16[192,4608]{1,0:T(8,128)(2,1)} %all-gather.3.cloned.1.call-done, bf16[4608,512]{1,0:T(8,128)(2,1)} %param.10), kind=kOutput, calls=%fused_computation.18 | convolution fusion | flops 905969664 | bytes 6881280 | tf_op jit(solution)/shard_map/dot_general | solution.py:34
  70.0 1.3 scatter_custom_fusion
  71.3 0.1 reduce_max.18
  71.4 39.4 %all-reduce.6 = (f32[192]{0:T(256)S(1)}, f32[192]{0:T(256)S(1)}) all-reduce(f32[192]{0:T(256)S(1)} %get-tuple-element.18, f32[192]{0:T(256)S(1)} %reduce_max.18), channel_id=1, replica_groups=mesh['dp'=8,'vocab'=4] {'dp','vocab'}, use_global_device_ids=true, to_apply=%region_8.9 | all-reduce | flops 384 | bytes 3072 | tf_op jit(solution)/shard_map/pmax | solution.py:43
  110.8 0.3 multiply_reduce_fusion
  111.1 41.0 %all-reduce.5 = (f32[192]{0:T(256)S(1)}, f32[192]{0:T(256)S(1)}) all-reduce(f32[192]{0:T(256)S(1)} %get-tuple-element.8, f32[192]{0:T(256)S(1)} %get-tuple-element.7), channel_id=1, replica_groups=mesh['dp'=8,'vocab'=4] {'dp','vocab'}, use_global_device_ids=true, to_apply=%region_10.11 | all-reduce | flops 384 | bytes 3072 | tf_op jit(solution)/shard_map/psum | solution.py:47
  152.1 0.2 select_convert_fusion
  152.3 3.4 %fusion.6 = f32[192,3584]{1,0:T(8,128)S(1)} fusion(bf16[192,512]{1,0:T(8,128)(2,1)S(1)} %select_convert_fusion, bf16[3584,512]{1,0:T(8,128)(2,1)} %param.9), kind=kOutput, calls=%fused_computation.19 | convolution fusion | flops 704643072 | bytes 6619136 | tf_op jit(solution)/shard_map/dot_general | solution.py:68
  155.7 75.6 %all-reduce.8 = (f32[192]{0:T(256)S(1)}, bf16[192,3584]{1,0:T(8,128)(2,1)}) all-reduce(f32[192]{0:T(256)S(1)} %get-tuple-element.6, f32[192,3584]{1,0:T(8,128)S(1)} %fusion.6), channel_id=1, replica_groups=mesh['dp'=8,'vocab'=4] {'dp','vocab'}, use_global_device_ids=true, to_apply=%region_4.5 | all-reduce | flops 688320 | bytes 4130304 | tf_op jit(solution)/shard_map/psum | solution.py:47
  231.3 0.6 select_reduce_fusion
  232.0 4.3 %fusion = bf16[3584,512]{0,1:T(8,128)(2,1)} fusion(bf16[192,512]{1,0:T(8,128)(2,1)S(1)} %select_convert_fusion, bf16[192,3584]{1,0:T(8,128)(2,1)} %all-gather.5.cloned.1.call-done), kind=kOutput, calls=%fused_computation.2 | convolution fusion | flops 706478080 | bytes 5242880 | tf_op jit(solution)/shard_map/dot_general | solution.py:63
  236.2 5.9 %copy.10 = bf16[3584,512]{1,0:T(8,128)(2,1)} copy(bf16[3584,512]{0,1:T(8,128)(2,1)} %fusion) | data formatting | bytes 7340032
  242.8 1.4 dynamic_slice.5
  (5 shorter events, 0.0 us)
Async XLA Ops:
  7.2 30.4 %all-gather.5.cloned.1.call-start = ((), (), s32[]{:S(2)}) async-start(), calls=%async_computation.1 | async-start | bytes 1548288 | tf_op jit(solution)/shard_map/all_gather | solution.py:31
  7.9 58.1 %all-gather.3.cloned.1.call-start = ((), (), s32[]{:S(2)}) async-start(), calls=%async_computation | async-start | bytes 1990656 | tf_op jit(solution)/shard_map/all_gather | solution.py:35
Sparse Core Ops, SparseCore 0:
  9.9 27.6 all-gather.4
  39.4 26.5 all-gather.2
where the time goes:
time: 253 us; the launch traced here: 252 us
  blocking collectives  165 us (65%)
  waiting for transfers between devices  39.9 us (16%)
  between operations  17.8 us (7%)
  matrix products  15.1 us (6%)
  local copies, waits for them, and re-layouts  12.4 us (5%)
    psum x2, blocking collectives, per_device(): lax.psum((jnp.sum(teacher_weights, axis=1), jnp.sum(jnp.exp(student_logit...  117 us
    pmax x1, blocking collectives, per_device(): lax.pmax((jnp.max(teacher_logits, axis=1), jnp.max(student_logits, axis=1...  39.4 us
    all_gather x1, waiting for transfers between devices, per_device(): lax.all_gather(teacher_hidden, 'dp', axis=0, tiled=True)  25 us
    all_gather x1, waiting for transfers between devices, per_device(): gathered = lax.all_gather(student_hidden, 'dp', axis=0, tiled=True)  13.6 us
    unnamed x8, local copies, waits for them, and re-layouts  9.52 us
    unnamed x1, blocking collectives  9.46 us
  transfers between devices with their start and end apart: 2, of which 2 were waited for; matrix products, arithmetic and copies ran while one was open for 3% of the time, Pallas kernels for 0%

commit v1 on v0

v1 whole, which is shorter than its diff:
```python
import functools

import jax
import jax.numpy as jnp
from jax import lax
from jax.experimental import pallas as pl
from jax.experimental.pallas import tpu as pltpu
from jax.sharding import PartitionSpec as P

loss_scale = 65536.0
MESH = pl.DeviceIdType.MESH


def nt(a, b):
    return lax.dot_general(a, b, (((1,), (1,)), ((), ())), preferred_element_type=jnp.float32)


def tn(a, b):
    return lax.dot_general(a, b, (((0,), (0,)), ((), ())), preferred_element_type=jnp.float32)


def nn(a, b):
    return jnp.dot(a, b, preferred_element_type=jnp.float32)


def merge(parts, count):
    t_top = parts[0, 0:1]
    s_top = parts[0, 1:2]
    for i in range(1, count):
        t_top = jnp.maximum(t_top, parts[i, 0:1])
        s_top = jnp.maximum(s_top, parts[i, 1:2])
    t_sum = jnp.zeros_like(t_top)
    s_sum = jnp.zeros_like(t_top)
    cross = jnp.zeros_like(t_top)
    for i in range(count):
        t_scale = jnp.exp(parts[i, 0:1] - t_top)
        t_sum += parts[i, 2:3] * t_scale
        cross += parts[i, 4:5] * t_scale
        s_sum += parts[i, 3:4] * jnp.exp(parts[i, 1:2] - s_top)
    return t_top, s_top, t_sum, s_sum, cross


def main_kernel(
    n, nv, rows, live, tiles,
    sh_ref, th_ref, meta_ref, shead_hbm, thead_hbm,
    loss_ref, hc_ref, lg_ref, gh_ref,
    gs, gt, gm, shead, thead, onehot_s, onehot_t, s_log, t_log,
    st, sz, lgx, core_out, core_in, mine, plane_out, plane_in, own, z_out, z_in,
    head_sem, m_send, m_recv, ici_send, core_send, g_recv,
    st_send, st_recv, sz_send, sz_recv, c_send, c_recv, p_send, p_recv, z_send, z_recv,
):
    nc = n // 2
    me = lax.axis_index("dp")
    vi = lax.axis_index("vocab")
    core = lax.rem(me, 2)
    chip = lax.div(me, 2)
    partner = 2 * chip + 1 - core
    pair = 2 * rows
    width = n * pair
    ds, dt = shead.shape[0], thead.shape[0]

    head_copies = [
        pltpu.make_async_copy(shead_hbm, shead, head_sem.at[0]),
        pltpu.make_async_copy(thead_hbm, thead, head_sem.at[1]),
    ]
    for copy in head_copies:
        copy.start()

    barrier = pltpu.get_barrier_semaphore()
    for r in range(1, n):
        pl.semaphore_signal(barrier, inc=1, device_id={"dp": lax.rem(me + r, n)}, device_id_type=MESH)
    for r in range(1, nv):
        pl.semaphore_signal(barrier, inc=1, device_id={"vocab": lax.rem(vi + r, nv)}, device_id_type=MESH)

    def folded(ref):
        half = ref.shape[1] // 2
        wide = ref[...].astype(jnp.float32)
        return jnp.concatenate([wide[:, :half], wide[:, half:]], axis=0).astype(jnp.bfloat16)

    gs[me] = folded(sh_ref)
    gt[me] = folded(th_ref)
    gm[me] = meta_ref[...]
    pl.semaphore_wait(barrier, n - 1 + nv - 1)

    def remote(src, dst, send, recv, target):
        return pltpu.make_async_remote_copy(
            src_ref=src, dst_ref=dst, send_sem=send, recv_sem=recv,
            device_id=target, device_id_type=MESH,
        )

    waits = []

    def go(copy):
        copy.start()
        waits.append(copy)

    for r in range(1, n):
        target = lax.rem(me + r, n)
        go(remote(gm.at[me], gm.at[me], m_send.at[r], m_recv.at[me], {"dp": target}))
    bufs = (gs, gt)
    for b, buf in enumerate(bufs):
        for r in range(1, nc):
            target = 2 * lax.rem(chip + r, nc) + core
            go(remote(buf.at[me], buf.at[me], ici_send.at[b, r], g_recv.at[b, me], {"dp": target}))
        go(remote(buf.at[me], buf.at[me], core_send.at[b, 0], g_recv.at[b, me], {"dp": partner}))

    def gather(b):
        buf = bufs[b]
        for r in range(1, nc):
            shard = 2 * lax.rem(chip + nc - r, nc) + core
            remote(buf.at[shard], buf.at[shard], core_send.at[b, r], g_recv.at[b, shard], {"dp": partner}).wait_recv()
            go(remote(buf.at[shard], buf.at[shard], core_send.at[b, r], g_recv.at[b, shard], {"dp": partner}))

    for r in range(1, n):
        shard = lax.rem(me + r, n)
        remote(gm.at[shard], gm.at[shard], m_send.at[r], m_recv.at[shard], {"dp": shard}).wait_recv()
    meta = gm[0]
    for i in range(1, n):
        meta = meta + gm[i]
    live_l, off_l, count_l, dest_l = meta[0:1], meta[1:2], meta[2:3], meta[3:4]

    lane = lax.broadcasted_iota(jnp.int32, (1, width), 1)
    half_l = jnp.zeros((1, width), jnp.int32)
    pos_l = lane
    for i in range(1, 2 * n):
        pos_l = jnp.where(lane >= i * rows, lane - i * rows, pos_l)
        if i % 2:
            half_l = jnp.where((lane >= i * rows) & (lane < (i + 1) * rows), 1, half_l)
    rank_l = jnp.zeros((1, width), jnp.int32)
    for i in range(n):
        off_i = off_l[:, i * pair:i * pair + 1]
        inside = (dest_l >= i * rows) & (dest_l < (i + 1) * rows)
        rank_l = jnp.where(inside, dest_l - i * rows + off_i, rank_l)
    shape = (2 * live, width)
    row = lax.broadcasted_iota(jnp.int32, shape, 0)
    key_s = jnp.where(pos_l < live_l, pos_l + off_l + live * half_l, -1)
    key_t = jnp.where(pos_l < count_l, rank_l + live * half_l, -1)
    onehot_s[...] = jnp.where(row == key_s, 1.0, 0.0).astype(jnp.bfloat16)
    onehot_t[...] = jnp.where(row == key_t, 1.0, 0.0).astype(jnp.bfloat16)

    def logits(b, onehot, head, out, keep, tile):
        buf = bufs[b]
        half = buf.shape[2]
        out[...] = jnp.zeros_like(out)

        def step(i, carry):
            at = pl.multiple_of(i * tile, 128)
            block = buf[:, :, pl.ds(at, tile)].reshape(width, tile)
            packed = nn(onehot[...], block).astype(jnp.bfloat16)
            top, low = packed[:live], packed[live:]
            if keep is not None:
                keep[:, pl.ds(at, tile)] = top
                keep[:, pl.ds(pl.multiple_of(half + at, 128), tile)] = low
            out[...] += nn(top, head[pl.ds(at, tile), :]) + nn(low, head[pl.ds(half + at, tile), :])
            return carry

        lax.fori_loop(0, half // tile, step, 0)

    def rest(b):
        buf = bufs[b]
        for r in range(nc):
            shard = 2 * lax.rem(chip + nc - r, nc) + 1 - core
            remote(buf.at[shard], buf.at[shard], core_send.at[b, r], g_recv.at[b, shard], {"dp": partner}).wait_recv()

    gather(0)
    rest(0)
    head_copies[0].wait()
    logits(0, onehot_s, shead, s_log, hc_ref, tiles[0])
    gather(1)
    rest(1)
    head_copies[1].wait()
    logits(1, onehot_t, thead, t_log, None, tiles[1])

    lanes = st.shape[2]
    s_val, t_val = s_log[...], t_log[...]
    t_top = jnp.max(t_val, axis=1, keepdims=True)
    s_top = jnp.max(s_val, axis=1, keepdims=True)
    t_exp = jnp.exp(t_val - t_top)
    t_sum = jnp.sum(t_exp, axis=1, keepdims=True)
    s_sum = jnp.sum(jnp.exp(s_val - s_top), axis=1, keepdims=True)
    cross = jnp.sum(t_exp * (t_val - s_val), axis=1, keepdims=True)
    col = lax.broadcasted_iota(jnp.int32, (live, 128), 1)
    table = jnp.where(col == 0, t_top, 1.0)
    for i, value in ((1, s_top), (2, t_sum), (3, s_sum), (4, cross)):
        table = jnp.where(col == i, value, table)
    if lanes > live:
        table = jnp.concatenate([table, jnp.ones((lanes - live, 128), jnp.float32)], axis=0)
    st[me] = jnp.transpose(table)[0:8]
    for r in range(1, n):
        go(remote(st.at[me], st.at[me], st_send.at[r], st_recv.at[me], {"dp": lax.rem(me + r, n)}))
    for r in range(1, n):
        shard = lax.rem(me + r, n)
        remote(st.at[shard], st.at[shard], st_send.at[r], st_recv.at[shard], {"dp": shard}).wait_recv()
    joined = merge(st, n)
    ones = jnp.ones((3, lanes), jnp.float32)
    sz[vi] = jnp.concatenate(list(joined) + [ones], axis=0)
    for r in range(1, nv):
        go(remote(sz.at[vi], sz.at[vi], sz_send.at[r], sz_recv.at[vi], {"vocab": lax.rem(vi + r, nv)}))
    for r in range(1, nv):
        shard = lax.rem(vi + r, nv)
        remote(sz.at[shard], sz.at[shard], sz_send.at[r], sz_recv.at[shard], {"vocab": shard}).wait_recv()
    t_top, s_top, t_sum, s_sum, cross = merge(sz, nv)
    t_norm = t_top + jnp.log(t_sum)
    s_norm = s_top + jnp.log(s_sum)
    divergence = cross / t_sum - t_norm + s_norm
    lane = lax.broadcasted_iota(jnp.int32, (1, lanes), 1)
    divergence = jnp.where(lane < live, divergence, 0.0)
    loss_ref[...] = jnp.sum(divergence, axis=1, keepdims=True) / live
    norms = jnp.concatenate([t_norm, s_norm, jnp.zeros((126, lanes), jnp.float32)], axis=0)
    norms = jnp.transpose(norms)[:live]
    gap = jnp.exp(s_val - norms[:, 1:2]) - jnp.exp(t_val - norms[:, 0:1])
    grad = (gap * (loss_scale / live)).astype(jnp.bfloat16)
    lg_ref[...] = grad

    spread = tn(onehot_s[0:live, :], grad)
    for k in range(2):
        lgx[k] = jnp.concatenate(
            [spread[(2 * c + k) * pair:(2 * c + k) * pair + rows] for c in range(nc)], axis=0
        ).astype(jnp.bfloat16)

    half = core_out.shape[3]

    def partial(k, v):
        base = pl.multiple_of(v * (2 * half), 16)
        low = nt(lgx[k], shead[pl.ds(base, half), :])
        high = nt(lgx[k], shead[pl.ds(pl.multiple_of(base + half, 16), half), :])
        return [
            jnp.concatenate([low[c * rows:(c + 1) * rows], high[c * rows:(c + 1) * rows]], axis=0)
            for c in range(nc)
        ]

    for j in range(nv):
        v = lax.rem(vi + 1 + j, nv)
        for c, block in enumerate(partial(1 - core, v)):
            core_out[j, c] = block.astype(jnp.bfloat16)
        go(remote(core_out.at[j], core_in.at[j], c_send.at[j], c_recv.at[j], {"dp": partner}))
        for c, block in enumerate(partial(core, v)):
            mine[j, c] = block
    for j in range(nv):
        remote(core_out.at[j], core_in.at[j], c_send.at[j], c_recv.at[j], {"dp": partner}).wait_recv()
        mine[j] = mine[j] + core_in[j].astype(jnp.float32)
        plane_out[j] = mine[j].astype(jnp.bfloat16)
        for r in range(1, nc):
            to = lax.rem(chip + r, nc)
            go(remote(plane_out.at[j, to], plane_in.at[j, r], p_send.at[j, r], p_recv.at[j, r], {"dp": 2 * to + core}))
    for j in range(nv):
        total = mine[j, chip]
        for r in range(1, nc):
            remote(plane_in.at[j, r], plane_in.at[j, r], p_send.at[j, r], p_recv.at[j, r], {"dp": partner}).wait_recv()
            total = total + plane_in[j, r].astype(jnp.float32)
        if j < nv - 1:
            z_out[j] = total.astype(jnp.bfloat16)
            go(remote(z_out.at[j], z_in.at[j], z_send.at[j], z_recv.at[j], {"vocab": lax.rem(vi + 1 + j, nv)}))
        else:
            own[...] = total
    total = own[...]
    for j in range(nv - 1):
        remote(z_in.at[j], z_in.at[j], z_send.at[j], z_recv.at[j], {"vocab": lax.rem(vi + 1, nv)}).wait_recv()
        total = total + z_in[j].astype(jnp.float32)
    gh_ref[...] = total.astype(jnp.bfloat16)
    for copy in waits:
        copy.wait_send()


def head_kernel(hc_ref, lg_ref, out_ref):
    out_ref[...] = tn(hc_ref[...], lg_ref[...]).astype(jnp.bfloat16)


def per_device(
    student_hidden,
    teacher_hidden,
    student_head,
    teacher_head,
    live_count,
    teacher_count,
    teacher_dest,
):
    rows, ds = student_hidden.shape
    dt = teacher_hidden.shape[1]
    vocab = student_head.shape[1]
    n = lax.axis_size("dp")
    nv = lax.axis_size("vocab")
    nc = n // 2
    live = rows * n // 2
    lanes = -(-live // 128) * 128
    pair = 2 * rows
    width = n * pair
    half = ds // nv // 2
    me = lax.axis_index("dp")

    lane_shard = lax.broadcasted_iota(jnp.int32, (width,), 0) // pair
    here = lane_shard == me
    dest = jnp.tile(teacher_dest, 2 * n)
    zero = jnp.zeros((width,), jnp.int32)
    meta = jnp.stack(
        [
            jnp.where(here, live_count[0], 0),
            jnp.where(lane_shard > me, live_count[0], 0),
            jnp.where(here, teacher_count[0], 0),
            jnp.where(here, dest, 0),
            zero, zero, zero, zero,
        ]
    )
    bf16, f32 = jnp.bfloat16, jnp.float32
    vmem = pl.BlockSpec(memory_space=pltpu.VMEM)
    hbm = pl.BlockSpec(memory_space=pl.ANY)
    dma = pltpu.SemaphoreType.DMA
    loss, hc, lg, gh = pl.pallas_call(
        functools.partial(main_kernel, n, nv, rows, live, (896, 768)),
        out_shape=(
            jax.ShapeDtypeStruct((1, 1), f32),
            jax.ShapeDtypeStruct((live, ds), bf16),
            jax.ShapeDtypeStruct((live, vocab), bf16),
            jax.ShapeDtypeStruct((pair, half), bf16),
        ),
        in_specs=[vmem, vmem, vmem, hbm, hbm],
        out_specs=(vmem, vmem, vmem, vmem),
        scratch_shapes=[
            pltpu.VMEM((n, pair, ds // 2), bf16),
            pltpu.VMEM((n, pair, dt // 2), bf16),
            pltpu.VMEM((n, 8, width), jnp.int32),
            pltpu.VMEM((ds, vocab), bf16),
            pltpu.VMEM((dt, vocab), bf16),
            pltpu.VMEM((2 * live, width), bf16),
            pltpu.VMEM((2 * live, width), bf16),
            pltpu.VMEM((live, vocab), f32),
            pltpu.VMEM((live, vocab), f32),
            pltpu.VMEM((n, 8, lanes), f32),
            pltpu.VMEM((nv, 8, lanes), f32),
            pltpu.VMEM((2, nc * rows, vocab), bf16),
            pltpu.VMEM((nv, nc, pair, half), bf16),
            pltpu.VMEM((nv, nc, pair, half), bf16),
            pltpu.VMEM((nv, nc, pair, half), f32),
            pltpu.VMEM((nv, nc, pair, half), bf16),
            pltpu.VMEM((nv, nc, pair, half), bf16),
            pltpu.VMEM((pair, half), f32),
            pltpu.VMEM((nv, pair, half), bf16),
            pltpu.VMEM((nv, pair, half), bf16),
            dma((2,)),
            dma((n,)), dma((n,)),
            dma((2, nc)), dma((2, nc)), dma((2, n)),
            dma((n,)), dma((n,)), dma((nv,)), dma((nv,)),
            dma((nv,)), dma((nv,)), dma((nv, nc)), dma((nv, nc)), dma((nv,)), dma((nv,)),
        ],
        compiler_params=pltpu.CompilerParams(
            collective_id=0, has_side_effects=True, vmem_limit_bytes=58 * 2**20
        ),
        name="distill",
    )(student_hidden, teacher_hidden, meta, student_head, teacher_head)
    tile = 512
    grad_head = pl.pallas_call(
        head_kernel,
        grid=(ds // tile,),
        out_shape=jax.ShapeDtypeStruct((ds, vocab), bf16),
        in_specs=[
            pl.BlockSpec((live, tile), lambda i: (0, i)),
            pl.BlockSpec((live, vocab), lambda i: (0, 0)),
        ],
        out_specs=pl.BlockSpec((tile, vocab), lambda i: (i, 0)),
        name="head_grad",
    )(hc, lg)
    grad_hidden = jnp.concatenate([gh[:rows], gh[rows:]], axis=1)
    return (loss[0, 0], grad_hidden, grad_head)


def solution(mesh):
    return jax.shard_map(
        per_device,
        mesh=mesh,
        in_specs=(
            P("dp", None),
            P("dp", None),
            P(None, ("dp", "vocab")),
            P(None, ("dp", "vocab")),
            P("dp"),
            P("dp"),
            P("dp"),
        ),
        out_specs=(P(), P("dp", "vocab"), P(None, ("dp", "vocab"))),
        check_vma=False,
    )
```

time: 253 us -> 66.2 us (0.26)
  blocking collectives: 165 us -> 0 us
  Pallas kernels: 0 us -> 59.2 us
  waiting for transfers between devices: 39.9 us -> 0 us
  matrix products: 15.1 us -> 0 us
  between operations: 17.8 us -> 3.76 us
  local copies, waits for them, and re-layouts: 12.4 us -> 2.13 us
    psum x2 -> x0, blocking collectives: 117 us -> none  [per_device(): lax.psum((jnp.sum(teacher_weights, axis=1), jnp.sum(jnp.exp(student_logit...]
    pallas_call x0 -> x2, Pallas kernels: none -> 59.2 us  [the longest x1 53.1 us: per_device(): pl.pallas_call(functools.partial(main_kernel, n, nv, rows, live, (896, 76...]
    pmax x1 -> x0, blocking collectives: 39.4 us -> none  [per_device(): lax.pmax((jnp.max(teacher_logits, axis=1), jnp.max(student_logits, axis=1...]
    all_gather x2 -> x0, waiting for transfers between devices: 38.5 us -> none  [the longest x1 25 us: per_device(): lax.all_gather(teacher_hidden, 'dp', axis=0, tiled=True)]
    dot_general x4 -> x0, matrix products: 15.1 us -> none  [the longest x1 4.29 us: per_device(): lax.dot_general(gathered, logit_grad, (((0,), (0,)), ((), ())), preferred...]
    unnamed x8 -> x0, local copies, waits for them, and re-layouts: 9.52 us -> none
    unnamed x1 -> x0, blocking collectives: 9.46 us -> none
  transfers between devices with their start and end apart: 2 -> 0, of which waited for: 2 -> 0; matrix products, arithmetic and copies ran while one was open for 3% -> 0% of each run, Pallas kernels for 0% -> 0%
where the time goes in v1:
time: 66.2 us; the launch traced here: 65.8 us
  Pallas kernels  59.2 us (89%)
  between operations  3.76 us (6%)
  local copies, waits for them, and re-layouts  2.13 us (3%)
  other arithmetic  0.73 us (1%)
    pallas_call x1, Pallas kernels, per_device(): pl.pallas_call(functools.partial(main_kernel, n, nv, rows, live, (896, 76...  53.1 us
    pallas_call x1, Pallas kernels, per_device(): pl.pallas_call(head_kernel, grid=(ds // tile,), out_shape=jax.ShapeDtypeS...  6.1 us

profile of v1, /device:TPU:0, one launch (start us, length us, event | category | flops | bytes accessed | tf_op | source)
XLA Modules:
  0.0 65.8 jit_solution(11713561275807206970)
XLA Ops:
  1.9 0.7 %tile.4 = s32[16,24]{1,0:T(8,128)S(1)} broadcast(s32[24]{0:T(128)} %param.13), dimensions={1} | broadcast | bytes 1632 | tf_op jit(solution)/shard_map/tile | solution.py:293
  2.6 0.1 tile.10
  2.7 0.6 stack.5.meta_ref
  3.4 53.1 %distill.1 = (f32[1,1]{1,0:T(1,128)}, bf16[96,3584]{1,0:T(8,128)(2,1)}, bf16[96,512]{1,0:T(8,128)(2,1)}, bf16[48,448]{1,0:T(8,128)(2,1)}) custom-call(bf16[24,3584]{1,0:T(8,128)(2,1)} %sh_ref.1, bf16[24,4608]{1,0:T(8,128)(2,1)} %th_ref.1, s32[8,384]{1,0:T(8,128)} %stack.5.meta_ref, bf16[3584,512]{1,0:T(8,128)(2,1)} %shead_hbm.1, bf16[4608,512]{1,0:T(8,128)(2,1)} %thead_hbm.1), custom_call_target="tpu_custom_call" | custom-call | tf_op jit(solution)/shard_map/distill/pallas_call | solution.py:308
  56.4 0.8 %fusion = (bf16[24,448]{1,0:T(8,128)(2,1)S(1)}, bf16[24,448]{1,0:T(8,128)(2,1)S(1)}) fusion(bf16[48,448]{1,0:T(8,128)(2,1)} %get-tuple-element.8), kind=kLoop, calls=%fused_computation.10 | loop fusion | bytes 86016 | tf_op jit(solution)/shard_map/slice | solution.py:362
  57.2 0.7 %pad_maximum_fusion = bf16[24,896]{1,0:T(8,128)(2,1)} fusion(bf16[24,448]{1,0:T(8,128)(2,1)S(1)} %get-tuple-element.12, bf16[24,448]{1,0:T(8,128)(2,1)S(1)} %get-tuple-element.11), kind=kLoop, calls=%fused_computation | loop fusion | flops 86016 | bytes 86016 | tf_op jit(solution)/shard_map/concatenate | solution.py:362
  57.9 6.1 %head_grad.1 = bf16[3584,512]{1,0:T(8,128)(2,1)} custom-call(bf16[96,3584]{1,0:T(8,128)(2,1)} %get-tuple-element.9.hc_ref, bf16[96,512]{1,0:T(8,128)(2,1)} %get-tuple-element.10.lg_ref), custom_call_target="tpu_custom_call" | custom-call | tf_op jit(solution)/shard_map/head_grad/pallas_call | solution.py:351
  (3 shorter events, 0.0 us)

commit v2 on v1

v2 whole, which is shorter than its diff:
```python
import functools

import jax
import jax.numpy as jnp
from jax import lax
from jax.experimental import pallas as pl
from jax.experimental.pallas import tpu as pltpu
from jax.sharding import PartitionSpec as P

loss_scale = 65536.0
MESH = pl.DeviceIdType.MESH


def nt(a, b):
    return lax.dot_general(a, b, (((1,), (1,)), ((), ())), preferred_element_type=jnp.float32)


def tn(a, b):
    return lax.dot_general(a, b, (((0,), (0,)), ((), ())), preferred_element_type=jnp.float32)


def nn(a, b):
    return jnp.dot(a, b, preferred_element_type=jnp.float32)


def merge(parts, count):
    t_top = parts[0, 0:1]
    s_top = parts[0, 1:2]
    for i in range(1, count):
        t_top = jnp.maximum(t_top, parts[i, 0:1])
        s_top = jnp.maximum(s_top, parts[i, 1:2])
    t_sum = jnp.zeros_like(t_top)
    s_sum = jnp.zeros_like(t_top)
    cross = jnp.zeros_like(t_top)
    for i in range(count):
        t_scale = jnp.exp(parts[i, 0:1] - t_top)
        t_sum += parts[i, 2:3] * t_scale
        cross += parts[i, 4:5] * t_scale
        s_sum += parts[i, 3:4] * jnp.exp(parts[i, 1:2] - s_top)
    return t_top, s_top, t_sum, s_sum, cross


def main_kernel(
    n, nv, rows, live, cuts, npieces,
    sh_ref, th_ref, live_ref, count_ref, dest_ref, shead_hbm, thead_hbm,
    loss_ref, ghead_ref, gh_ref, *scratch,
):
    bufs, scratch = scratch[:npieces], scratch[npieces:]
    (
        gm, shead, thead, onehot_s, onehot_t, hc_ref, s_log, t_log,
        st, sz, lgx, core_out, core_in, mine, plane_out, plane_in, own, z_out, z_in,
        head_sem, m_send, m_recv, ici_send, core_send, g_recv, relay_send, relay_recv,
        st_send, st_recv, sz_send, sz_recv, c_send, c_recv, p_send, p_recv, z_send, z_recv,
    ) = scratch
    nc = n // 2
    me = lax.axis_index("dp")
    vi = lax.axis_index("vocab")
    core = lax.rem(me, 2)
    chip = lax.div(me, 2)
    partner = 2 * chip + 1 - core
    pair = 2 * rows
    width = n * pair
    ds, dt = shead.shape[0], thead.shape[0]

    head_copies = [
        pltpu.make_async_copy(shead_hbm, shead, head_sem.at[0]),
        pltpu.make_async_copy(thead_hbm, thead, head_sem.at[1]),
    ]
    for copy in head_copies:
        copy.start()

    barrier = pltpu.get_barrier_semaphore()
    for r in range(1, n):
        pl.semaphore_signal(barrier, inc=1, device_id={"dp": lax.rem(me + r, n)}, device_id_type=MESH)
    for r in range(1, nv):
        pl.semaphore_signal(barrier, inc=1, device_id={"vocab": lax.rem(vi + r, nv)}, device_id_type=MESH)

    lane = lax.broadcasted_iota(jnp.int32, (1, width), 1)
    half_l = jnp.zeros((1, width), jnp.int32)
    shard_l = jnp.zeros((1, width), jnp.int32)
    pos_l = lane
    for i in range(1, 2 * n):
        pos_l = jnp.where(lane >= i * rows, lane - i * rows, pos_l)
        half_l = jnp.where(lane >= i * rows, i % 2, half_l)
        shard_l = jnp.where(lane >= i * rows, i // 2, shard_l)
    dest_l = jnp.zeros((1, width), jnp.int32)
    for i in range(rows):
        dest_l = jnp.where(pos_l == i, dest_ref[i], dest_l)
    here = shard_l == me
    gm[me] = jnp.concatenate(
        [
            jnp.where(here, live_ref[0], 0),
            jnp.where(shard_l > me, live_ref[0], 0),
            jnp.where(here, count_ref[0], 0),
            jnp.where(here, dest_l, 0),
            jnp.zeros((4, width), jnp.int32),
        ],
        axis=0,
    )
    for i, (b, at, size) in enumerate(cuts):
        ref = (sh_ref, th_ref)[b]
        half = ref.shape[1] // 2
        left = ref[:, at:at + size].astype(jnp.float32)
        right = ref[:, half + at:half + at + size].astype(jnp.float32)
        bufs[i][me] = jnp.concatenate([left, right], axis=0).astype(jnp.bfloat16)
    pl.semaphore_wait(barrier, n - 1 + nv - 1)

    def remote(src, dst, send, recv, target):
        return pltpu.make_async_remote_copy(
            src_ref=src, dst_ref=dst, send_sem=send, recv_sem=recv,
            device_id=target, device_id_type=MESH,
        )

    waits = []

    def go(copy):
        copy.start()
        waits.append(copy)

    for r in range(1, n):
        target = lax.rem(me + r, n)
        go(remote(gm.at[me], gm.at[me], m_send.at[r], m_recv.at[me], {"dp": target}))
    square = nc == 4
    x_chip = 2 * lax.div(chip, 2) + 1 - lax.rem(chip, 2)
    y_chip = lax.rem(chip + 2, 4)
    targets = [x_chip, y_chip] if square else [lax.rem(chip + r, nc) for r in range(1, nc)]
    sources = [x_chip, y_chip] if square else [lax.rem(chip + nc - r, nc) for r in range(1, nc)]

    def block_copy(i, shard, send, target):
        return remote(bufs[i].at[shard], bufs[i].at[shard], send, g_recv.at[i, shard], {"dp": target})

    def start_own(i):
        for r, to in enumerate(targets):
            go(block_copy(i, me, ici_send.at[i, r], 2 * to + core))
        go(block_copy(i, me, core_send.at[i, 0], partner))

    def pass_on(i):
        for r, source in enumerate(sources):
            shard = 2 * source + core
            block_copy(i, shard, core_send.at[i, r + 1], partner).wait_recv()
            if square:
                size = bufs[i].shape[2] // 2
                to = (y_chip, x_chip)[r]
                part = bufs[i].at[shard, :, pl.ds(r * size, size)]
                go(remote(part, part, relay_send.at[i, r], relay_recv.at[i, r], {"dp": 2 * to + core}))
            go(block_copy(i, shard, core_send.at[i, r + 1], partner))

    def finish(i):
        if square:
            shard = 2 * (3 - chip) + core
            for r in range(2):
                size = bufs[i].shape[2] // 2
                part = bufs[i].at[shard, :, pl.ds(r * size, size)]
                remote(part, part, relay_send.at[i, r], relay_recv.at[i, r], {"dp": partner}).wait_recv()
            go(block_copy(i, shard, core_send.at[i, 3], partner))
        for c in range(nc):
            block_copy(i, 2 * c + 1 - core, core_send.at[i, 0], partner).wait_recv()

    start_own(0)
    start_own(1)
    for r in range(1, n):
        shard = lax.rem(me + r, n)
        remote(gm.at[shard], gm.at[shard], m_send.at[r], m_recv.at[shard], {"dp": shard}).wait_recv()
    meta = gm[0]
    for i in range(1, n):
        meta = meta + gm[i]
    live_l, off_l, count_l, dest_l = meta[0:1], meta[1:2], meta[2:3], meta[3:4]

    rank_l = jnp.zeros((1, width), jnp.int32)
    for i in range(n):
        off_i = off_l[:, i * pair:i * pair + 1]
        inside = (dest_l >= i * rows) & (dest_l < (i + 1) * rows)
        rank_l = jnp.where(inside, dest_l - i * rows + off_i, rank_l)
    shape = (2 * live, width)
    row = lax.broadcasted_iota(jnp.int32, shape, 0)
    key_s = jnp.where(pos_l < live_l, pos_l + off_l + live * half_l, -1)
    key_t = jnp.where(pos_l < count_l, rank_l + live * half_l, -1)
    onehot_s[...] = jnp.where(row == key_s, 1.0, 0.0).astype(jnp.bfloat16)
    onehot_t[...] = jnp.where(row == key_t, 1.0, 0.0).astype(jnp.bfloat16)

    def logits(i):
        b, at, size = cuts[i]
        onehot, head, out = ((onehot_s, shead, s_log), (onehot_t, thead, t_log))[b]
        half = head.shape[0] // 2
        packed = nn(onehot[...], bufs[i][...].reshape(width, size)).astype(jnp.bfloat16)
        top, low = packed[:live], packed[live:]
        if b == 0:
            hc_ref[:, at:at + size] = top
            hc_ref[:, half + at:half + at + size] = low
        value = nn(top, head[at:at + size, :]) + nn(low, head[half + at:half + at + size, :])
        out[...] = value if at == 0 else out[...] + value

    for i in range(npieces + 1):
        if i < npieces:
            pass_on(i)
            if i + 2 < npieces:
                start_own(i + 2)
        if i >= 1:
            finish(i - 1)
            b, at, _ = cuts[i - 1]
            if at == 0:
                head_copies[b].wait()
            logits(i - 1)

    lanes = st.shape[2]
    s_val, t_val = s_log[...], t_log[...]
    t_top = jnp.max(t_val, axis=1, keepdims=True)
    s_top = jnp.max(s_val, axis=1, keepdims=True)
    t_exp = jnp.exp(t_val - t_top)
    t_sum = jnp.sum(t_exp, axis=1, keepdims=True)
    s_sum = jnp.sum(jnp.exp(s_val - s_top), axis=1, keepdims=True)
    cross = jnp.sum(t_exp * (t_val - s_val), axis=1, keepdims=True)
    col = lax.broadcasted_iota(jnp.int32, (live, 128), 1)
    table = jnp.where(col == 0, t_top, 1.0)
    for i, value in ((1, s_top), (2, t_sum), (3, s_sum), (4, cross)):
        table = jnp.where(col == i, value, table)
    if lanes > live:
        table = jnp.concatenate([table, jnp.ones((lanes - live, 128), jnp.float32)], axis=0)
    st[me] = jnp.transpose(table)[0:8]
    for r in range(1, n):
        go(remote(st.at[me], st.at[me], st_send.at[r], st_recv.at[me], {"dp": lax.rem(me + r, n)}))
    for r in range(1, n):
        shard = lax.rem(me + r, n)
        remote(st.at[shard], st.at[shard], st_send.at[r], st_recv.at[shard], {"dp": shard}).wait_recv()
    joined = merge(st, n)
    ones = jnp.ones((3, lanes), jnp.float32)
    sz[vi] = jnp.concatenate(list(joined) + [ones], axis=0)
    for r in range(1, nv):
        go(remote(sz.at[vi], sz.at[vi], sz_send.at[r], sz_recv.at[vi], {"vocab": lax.rem(vi + r, nv)}))
    for r in range(1, nv):
        shard = lax.rem(vi + r, nv)
        remote(sz.at[shard], sz.at[shard], sz_send.at[r], sz_recv.at[shard], {"vocab": shard}).wait_recv()
    t_top, s_top, t_sum, s_sum, cross = merge(sz, nv)
    t_norm = t_top + jnp.log(t_sum)
    s_norm = s_top + jnp.log(s_sum)
    divergence = cross / t_sum - t_norm + s_norm
    lane = lax.broadcasted_iota(jnp.int32, (1, lanes), 1)
    divergence = jnp.where(lane < live, divergence, 0.0)
    loss_ref[...] = jnp.sum(divergence, axis=1, keepdims=True) / live
    norms = jnp.concatenate([t_norm, s_norm, jnp.zeros((126, lanes), jnp.float32)], axis=0)
    norms = jnp.transpose(norms)[:live]
    gap = jnp.exp(s_val - norms[:, 1:2]) - jnp.exp(t_val - norms[:, 0:1])
    grad = (gap * (loss_scale / live)).astype(jnp.bfloat16)

    spread = tn(onehot_s[0:live, :], grad)
    sides = [
        jnp.concatenate([spread[(2 * c + k) * pair:(2 * c + k) * pair + rows] for c in range(nc)], axis=0)
        for k in range(2)
    ]
    is_zero = core == 0
    lgx[0:nc * rows] = jnp.where(is_zero, sides[1], sides[0]).astype(jnp.bfloat16)
    lgx[nc * rows:] = jnp.where(is_zero, sides[0], sides[1]).astype(jnp.bfloat16)

    half = core_out.shape[3]

    for j in range(nv):
        base = pl.multiple_of(lax.rem(vi + 1 + j, nv) * (2 * half), 16)
        low = nt(lgx[...], shead[pl.ds(base, half), :])
        high = nt(lgx[...], shead[pl.ds(pl.multiple_of(base + half, 16), half), :])
        blocks = [
            jnp.concatenate([low[c * rows:(c + 1) * rows], high[c * rows:(c + 1) * rows]], axis=0)
            for c in range(2 * nc)
        ]
        for c in range(nc):
            core_out[j, c] = blocks[c].astype(jnp.bfloat16)
        go(remote(core_out.at[j], core_in.at[j], c_send.at[j], c_recv.at[j], {"dp": partner}))
        for c in range(nc):
            mine[j, c] = blocks[nc + c]
    for j in range(nv):
        remote(core_out.at[j], core_in.at[j], c_send.at[j], c_recv.at[j], {"dp": partner}).wait_recv()
        mine[j] = mine[j] + core_in[j].astype(jnp.float32)
        plane_out[j] = mine[j].astype(jnp.bfloat16)
        for r in range(1, nc):
            to = lax.rem(chip + r, nc)
            go(remote(plane_out.at[j, to], plane_in.at[j, r], p_send.at[j, r], p_recv.at[j, r], {"dp": 2 * to + core}))
    tile = 512
    slabs = ds // tile
    for j in range(nv):
        for i in range(slabs * j // nv, slabs * (j + 1) // nv):
            ghead_ref[i * tile:(i + 1) * tile, :] = tn(hc_ref[:, i * tile:(i + 1) * tile], grad).astype(jnp.bfloat16)
        total = mine[j, chip]
        for r in range(1, nc):
            remote(plane_in.at[j, r], plane_in.at[j, r], p_send.at[j, r], p_recv.at[j, r], {"dp": partner}).wait_recv()
            total = total + plane_in[j, r].astype(jnp.float32)
        if j < nv - 1:
            z_out[j] = total.astype(jnp.bfloat16)
            go(remote(z_out.at[j], z_in.at[j], z_send.at[j], z_recv.at[j], {"vocab": lax.rem(vi + 1 + j, nv)}))
        else:
            own[...] = total
    total = own[...]
    for j in range(nv - 1):
        remote(z_in.at[j], z_in.at[j], z_send.at[j], z_recv.at[j], {"vocab": lax.rem(vi + 1, nv)}).wait_recv()
        total = total + z_in[j].astype(jnp.float32)
    gh_ref[...] = total.astype(jnp.bfloat16)
    for copy in waits:
        copy.wait_send()


def per_device(
    student_hidden,
    teacher_hidden,
    student_head,
    teacher_head,
    live_count,
    teacher_count,
    teacher_dest,
):
    rows, ds = student_hidden.shape
    dt = teacher_hidden.shape[1]
    vocab = student_head.shape[1]
    n = lax.axis_size("dp")
    nv = lax.axis_size("vocab")
    nc = n // 2
    live = rows * n // 2
    lanes = -(-live // 128) * 128
    pair = 2 * rows
    width = n * pair
    half = ds // nv // 2
    bf16, f32 = jnp.bfloat16, jnp.float32
    vmem = pl.BlockSpec(memory_space=pltpu.VMEM)
    hbm = pl.BlockSpec(memory_space=pltpu.HBM)
    dma = pltpu.SemaphoreType.DMA
    smem = pl.BlockSpec(memory_space=pltpu.SMEM)
    cuts = []
    for b, sizes in enumerate(((1024, 768), (768, 768, 768))):
        at = 0
        for size in sizes:
            cuts.append((b, at, size))
            at += size
        assert at == (ds, dt)[b] // 2
    pieces = len(cuts)
    loss, grad_head, gh = pl.pallas_call(
        functools.partial(main_kernel, n, nv, rows, live, cuts, pieces),
        out_shape=(
            jax.ShapeDtypeStruct((1, 1), f32),
            pltpu.VMEM((ds, vocab), bf16),
            jax.ShapeDtypeStruct((pair, half), bf16),
        ),
        in_specs=[vmem, vmem, smem, smem, smem, hbm, hbm],
        out_specs=(vmem, vmem, vmem),
        scratch_shapes=[
            *[pltpu.VMEM((n, pair, size), bf16) for _, _, size in cuts],
            pltpu.VMEM((n, 8, width), jnp.int32),
            pltpu.VMEM((ds, vocab), bf16),
            pltpu.VMEM((dt, vocab), bf16),
            pltpu.VMEM((2 * live, width), bf16),
            pltpu.VMEM((2 * live, width), bf16),
            pltpu.VMEM((live, ds), bf16),
            pltpu.VMEM((live, vocab), f32),
            pltpu.VMEM((live, vocab), f32),
            pltpu.VMEM((n, 8, lanes), f32),
            pltpu.VMEM((nv, 8, lanes), f32),
            pltpu.VMEM((2 * nc * rows, vocab), bf16),
            pltpu.VMEM((nv, nc, pair, half), bf16),
            pltpu.VMEM((nv, nc, pair, half), bf16),
            pltpu.VMEM((nv, nc, pair, half), f32),
            pltpu.VMEM((nv, nc, pair, half), bf16),
            pltpu.VMEM((nv, nc, pair, half), bf16),
            pltpu.VMEM((pair, half), f32),
            pltpu.VMEM((nv, pair, half), bf16),
            pltpu.VMEM((nv, pair, half), bf16),
            dma((2,)),
            dma((n,)), dma((n,)),
            dma((pieces, nc)), dma((pieces, nc)), dma((pieces, n)), dma((pieces, 2)), dma((pieces, 2)),
            dma((n,)), dma((n,)), dma((nv,)), dma((nv,)),
            dma((nv,)), dma((nv,)), dma((nv, nc)), dma((nv, nc)), dma((nv,)), dma((nv,)),
        ],
        compiler_params=pltpu.CompilerParams(
            collective_id=0, has_side_effects=True, vmem_limit_bytes=(56 if n <= 8 else 58) * 2**20
        ),
        name="distill",
    )(student_hidden, teacher_hidden, live_count, teacher_count, teacher_dest, student_head, teacher_head)
    grad_hidden = jnp.concatenate([gh[:rows], gh[rows:]], axis=1)
    return (loss[0, 0], grad_hidden, grad_head)


def solution(mesh):
    return jax.shard_map(
        per_device,
        mesh=mesh,
        in_specs=(
            P("dp", None),
            P("dp", None),
            P(None, ("dp", "vocab")),
            P(None, ("dp", "vocab")),
            P("dp"),
            P("dp"),
            P("dp"),
        ),
        out_specs=(P(), P("dp", "vocab"), P(None, ("dp", "vocab"))),
        check_vma=False,
    )
```

time: 66.2 us -> 56.4 us (0.85)
  Pallas kernels: 59.2 us -> 49.2 us
    pallas_call x2 -> x1, Pallas kernels: 59.2 us -> 49.2 us  [per_device(): pl.pallas_call(functools.partial(main_kernel, n, nv, rows, live, cuts, pi...]
    unnamed x0 -> x1, local copies, waits for them, and re-layouts: none -> 1.84 us
    another operation x4 -> x0, local copies, waits for them, and re-layouts: 1.37 us -> none  [the longest x2 0.74 us: per_device(): dest = jnp.tile(teacher_dest, 2 * n)]
where the time goes in v2:
time: 56.4 us; the launch traced here: 56.1 us
  Pallas kernels  49.2 us (87%)
  between operations  3.68 us (7%)
  local copies, waits for them, and re-layouts  2.6 us (5%)
  other arithmetic  0.7 us (1%)
    pallas_call x1, Pallas kernels, per_device(): pl.pallas_call(functools.partial(main_kernel, n, nv, rows, live, cuts, pi...  49.2 us
    unnamed x1, local copies, waits for them, and re-layouts  1.84 us

profile of v2, /device:TPU:0, one launch (start us, length us, event | category | flops | bytes accessed | tf_op | source)
XLA Modules:
  0.0 56.1 jit_solution(10803389074234702009)
XLA Ops:
  1.9 49.2 %distill.1 = (f32[1,1]{1,0:T(1,128)}, bf16[3584,512]{1,0:T(8,128)(2,1)S(1)}, bf16[48,448]{1,0:T(8,128)(2,1)}) custom-call(bf16[24,3584]{1,0:T(8,128)(2,1)} %sh_ref.1, bf16[24,4608]{1,0:T(8,128)(2,1)} %th_ref.1, s32[1]{0:T(128)S(6)} %copy.13.live_ref, s32[1]{0:T(128)S(6)} %copy.14.count_ref, s32[24]{0:T(128)} %dest_ref.1, bf16[3584,512]{1,0:T(8,128)(2,1)} %shead_hbm.1, ...), custom_call_target="tpu_custom_call" | custom-call | tf_op jit(solution)/shard_map/distill/pallas_call | solution.py:332
  51.1 0.8 %fusion = (bf16[24,448]{1,0:T(8,128)(2,1)S(1)}, bf16[24,448]{1,0:T(8,128)(2,1)S(1)}) fusion(bf16[48,448]{1,0:T(8,128)(2,1)} %get-tuple-element.7), kind=kLoop, calls=%fused_computation.1 | loop fusion | bytes 86016 | tf_op jit(solution)/shard_map/slice | solution.py:373
  51.8 0.7 %pad_maximum_fusion = bf16[24,896]{1,0:T(8,128)(2,1)} fusion(bf16[24,448]{1,0:T(8,128)(2,1)S(1)} %get-tuple-element.10, bf16[24,448]{1,0:T(8,128)(2,1)S(1)} %get-tuple-element.9), kind=kLoop, calls=%fused_computation | loop fusion | flops 86016 | bytes 86016 | tf_op jit(solution)/shard_map/concatenate | solution.py:373
  52.5 1.8 %copy.12 = bf16[3584,512]{1,0:T(8,128)(2,1)} copy(bf16[3584,512]{1,0:T(8,128)(2,1)S(1)} %get-tuple-element.13) | data formatting | bytes 7340032

commit v3 on v2

--- a/solution.py
+++ b/solution.py
@@ -74,6 +74,14 @@
         pl.semaphore_signal(barrier, inc=1, device_id={"dp": lax.rem(me + r, n)}, device_id_type=MESH)
     for r in range(1, nv):
         pl.semaphore_signal(barrier, inc=1, device_id={"vocab": lax.rem(vi + r, nv)}, device_id_type=MESH)
+
+    def fold(i):
+        b, at, size = cuts[i]
+        ref = (sh_ref, th_ref)[b]
+        half = ref.shape[1] // 2
+        left = ref[:, at:at + size].astype(jnp.float32)
+        right = ref[:, half + at:half + at + size].astype(jnp.float32)
+        bufs[i][me] = jnp.concatenate([left, right], axis=0).astype(jnp.bfloat16)
 
     lane = lax.broadcasted_iota(jnp.int32, (1, width), 1)
     half_l = jnp.zeros((1, width), jnp.int32)
@@ -97,12 +105,8 @@
         ],
         axis=0,
     )
-    for i, (b, at, size) in enumerate(cuts):
-        ref = (sh_ref, th_ref)[b]
-        half = ref.shape[1] // 2
-        left = ref[:, at:at + size].astype(jnp.float32)
-        right = ref[:, half + at:half + at + size].astype(jnp.float32)
-        bufs[i][me] = jnp.concatenate([left, right], axis=0).astype(jnp.bfloat16)
+    fold(0)
+    fold(1)
     pl.semaphore_wait(barrier, n - 1 + nv - 1)
 
     def remote(src, dst, send, recv, target):
@@ -117,9 +121,6 @@
         copy.start()
         waits.append(copy)
 
-    for r in range(1, n):
-        target = lax.rem(me + r, n)
-        go(remote(gm.at[me], gm.at[me], m_send.at[r], m_recv.at[me], {"dp": target}))
     square = nc == 4
     x_chip = 2 * lax.div(chip, 2) + 1 - lax.rem(chip, 2)
     y_chip = lax.rem(chip + 2, 4)
@@ -156,8 +157,15 @@
         for c in range(nc):
             block_copy(i, 2 * c + 1 - core, core_send.at[i, 0], partner).wait_recv()
 
+    for r in range(1, n):
+        target = lax.rem(me + r, n)
+        go(remote(gm.at[me], gm.at[me], m_send.at[r], m_recv.at[me], {"dp": target}))
     start_own(0)
     start_own(1)
+    for i in range(2, npieces):
+        fold(i)
+    pass_on(0)
+    start_own(2)
     for r in range(1, n):
         shard = lax.rem(me + r, n)
         remote(gm.at[shard], gm.at[shard], m_send.at[r], m_recv.at[shard], {"dp": shard}).wait_recv()
@@ -191,7 +199,7 @@
         out[...] = value if at == 0 else out[...] + value
 
     for i in range(npieces + 1):
-        if i < npieces:
+        if 0 < i < npieces:
             pass_on(i)
             if i + 2 < npieces:
                 start_own(i + 2)
@@ -253,7 +261,7 @@
 
     half = core_out.shape[3]
 
-    for j in range(nv):
+    def partial(j):
         base = pl.multiple_of(lax.rem(vi + 1 + j, nv) * (2 * half), 16)
         low = nt(lgx[...], shead[pl.ds(base, half), :])
         high = nt(lgx[...], shead[pl.ds(pl.multiple_of(base + half, 16), half), :])
@@ -266,13 +274,20 @@
         go(remote(core_out.at[j], core_in.at[j], c_send.at[j], c_recv.at[j], {"dp": partner}))
         for c in range(nc):
             mine[j, c] = blocks[nc + c]
-    for j in range(nv):
+
+    def to_plane(j):
         remote(core_out.at[j], core_in.at[j], c_send.at[j], c_recv.at[j], {"dp": partner}).wait_recv()
         mine[j] = mine[j] + core_in[j].astype(jnp.float32)
         plane_out[j] = mine[j].astype(jnp.bfloat16)
         for r in range(1, nc):
             to = lax.rem(chip + r, nc)
             go(remote(plane_out.at[j, to], plane_in.at[j, r], p_send.at[j, r], p_recv.at[j, r], {"dp": 2 * to + core}))
+
+    for j in range(nv + 1):
+        if j < nv:
+            partial(j)
+        if j >= 1:
+            to_plane(j - 1)
     tile = 512
     slabs = ds // tile
     for j in range(nv):
@@ -291,7 +306,7 @@
     for j in range(nv - 1):
         remote(z_in.at[j], z_in.at[j], z_send.at[j], z_recv.at[j], {"vocab": lax.rem(vi + 1, nv)}).wait_recv()
         total = total + z_in[j].astype(jnp.float32)
-    gh_ref[...] = total.astype(jnp.bfloat16)
+    gh_ref[...] = jnp.concatenate([total[:rows], total[rows:]], axis=1).astype(jnp.bfloat16)
     for copy in waits:
         copy.wait_send()
 
@@ -329,12 +344,12 @@
             at += size
         assert at == (ds, dt)[b] // 2
     pieces = len(cuts)
-    loss, grad_head, gh = pl.pallas_call(
+    loss, grad_head, grad_hidden = pl.pallas_call(
         functools.partial(main_kernel, n, nv, rows, live, cuts, pieces),
         out_shape=(
             jax.ShapeDtypeStruct((1, 1), f32),
             pltpu.VMEM((ds, vocab), bf16),
-            jax.ShapeDtypeStruct((pair, half), bf16),
+            pltpu.VMEM((rows, 2 * half), bf16),
         ),
         in_specs=[vmem, vmem, smem, smem, smem, hbm, hbm],
         out_specs=(vmem, vmem, vmem),
@@ -370,7 +385,6 @@
         ),
         name="distill",
     )(student_hidden, teacher_hidden, live_count, teacher_count, teacher_dest, student_head, teacher_head)
-    grad_hidden = jnp.concatenate([gh[:rows], gh[rows:]], axis=1)
     return (loss[0, 0], grad_hidden, grad_head)
 
 

time: 56.4 us -> 54.8 us (0.972)
  Pallas kernels: 49.2 us -> 48.5 us
  other arithmetic: 0.7 us -> 0 us
    slice x1 -> x0, local copies, waits for them, and re-layouts: 0.76 us -> none  [per_device(): grad_hidden = jnp.concatenate([gh[:rows], gh[rows:]], axis=1)]
    concatenate x1 -> x0, other arithmetic: 0.7 us -> none  [per_device(): grad_hidden = jnp.concatenate([gh[:rows], gh[rows:]], axis=1)]
    pallas_call x1, Pallas kernels: 49.2 us -> 48.5 us  [per_device(): pl.pallas_call(functools.partial(main_kernel, n, nv, rows, live, cuts, pi...]
    unnamed x1 -> x2, local copies, waits for them, and re-layouts: 1.84 us -> 2.46 us
where the time goes in v3:
time: 54.8 us; the launch traced here: 54.6 us
  Pallas kernels  48.5 us (89%)
  between operations  3.62 us (7%)
  local copies, waits for them, and re-layouts  2.46 us (4%)
    pallas_call x1, Pallas kernels, per_device(): pl.pallas_call(functools.partial(main_kernel, n, nv, rows, live, cuts, pi...  48.5 us
    unnamed x2, local copies, waits for them, and re-layouts  2.46 us

profile of v3, /device:TPU:0, one launch (start us, length us, event | category | flops | bytes accessed | tf_op | source)
XLA Modules:
  0.0 54.6 jit_solution(4011024773562001026)
XLA Ops:
  1.9 48.5 %distill.1 = (f32[1,1]{1,0:T(1,128)}, bf16[3584,512]{1,0:T(8,128)(2,1)S(1)}, bf16[24,896]{1,0:T(8,128)(2,1)S(1)}) custom-call(bf16[24,3584]{1,0:T(8,128)(2,1)} %sh_ref.1, bf16[24,4608]{1,0:T(8,128)(2,1)} %th_ref.1, s32[1]{0:T(128)S(6)} %copy.15.live_ref, s32[1]{0:T(128)S(6)} %copy.16.count_ref, s32[24]{0:T(128)} %dest_ref.1, bf16[3584,512]{1,0:T(8,128)(2,1)} %shead_hbm.1, ...), custom_call_target="tpu_custom_call" | custom-call | tf_op jit(solution)/shard_map/distill/pallas_call | solution.py:347
  50.4 0.6 %copy.13 = bf16[24,896]{1,0:T(8,128)(2,1)} copy(bf16[24,896]{1,0:T(8,128)(2,1)S(1)} %get-tuple-element.10) | data formatting | bytes 86016
  51.1 1.8 %copy.14 = bf16[3584,512]{1,0:T(8,128)(2,1)} copy(bf16[3584,512]{1,0:T(8,128)(2,1)S(1)} %get-tuple-element.11) | data formatting | bytes 7340032

commit v4 on v3

--- a/solution.py
+++ b/solution.py
@@ -47,7 +47,7 @@
 ):
     bufs, scratch = scratch[:npieces], scratch[npieces:]
     (
-        gm, shead, thead, onehot_s, onehot_t, hc_ref, s_log, t_log,
+        gm, shead, thead, onehot_s, onehot_t, hc_ref, hct, s_log, t_log,
         st, sz, lgx, core_out, core_in, mine, plane_out, plane_in, own, z_out, z_in,
         head_sem, m_send, m_recv, ici_send, core_send, g_recv, relay_send, relay_recv,
         st_send, st_recv, sz_send, sz_recv, c_send, c_recv, p_send, p_recv, z_send, z_recv,
@@ -117,9 +117,11 @@
 
     waits = []
 
-    def go(copy):
+    late = []
+
+    def go(copy, kept=waits):
         copy.start()
-        waits.append(copy)
+        kept.append(copy)
 
     square = nc == 4
     x_chip = 2 * lax.div(chip, 2) + 1 - lax.rem(chip, 2)
@@ -227,6 +229,14 @@
     st[me] = jnp.transpose(table)[0:8]
     for r in range(1, n):
         go(remote(st.at[me], st.at[me], st_send.at[r], st_recv.at[me], {"dp": lax.rem(me + r, n)}))
+    tile = 512
+    slabs = ds // tile
+
+    def turn(first, last):
+        for i in range(first, last):
+            hct[i * tile:(i + 1) * tile, :] = jnp.transpose(hc_ref[:, i * tile:(i + 1) * tile])
+
+    turn(0, slabs // 2)
     for r in range(1, n):
         shard = lax.rem(me + r, n)
         remote(st.at[shard], st.at[shard], st_send.at[r], st_recv.at[shard], {"dp": shard}).wait_recv()
@@ -235,6 +245,7 @@
     sz[vi] = jnp.concatenate(list(joined) + [ones], axis=0)
     for r in range(1, nv):
         go(remote(sz.at[vi], sz.at[vi], sz_send.at[r], sz_recv.at[vi], {"vocab": lax.rem(vi + r, nv)}))
+    turn(slabs // 2, slabs)
     for r in range(1, nv):
         shard = lax.rem(vi + r, nv)
         remote(sz.at[shard], sz.at[shard], sz_send.at[r], sz_recv.at[shard], {"vocab": shard}).wait_recv()
@@ -281,25 +292,26 @@
         plane_out[j] = mine[j].astype(jnp.bfloat16)
         for r in range(1, nc):
             to = lax.rem(chip + r, nc)
-            go(remote(plane_out.at[j, to], plane_in.at[j, r], p_send.at[j, r], p_recv.at[j, r], {"dp": 2 * to + core}))
+            go(remote(plane_out.at[j, to], plane_in.at[j, r], p_send.at[j, r], p_recv.at[j, r], {"dp": 2 * to + core}), late)
 
     for j in range(nv + 1):
         if j < nv:
             partial(j)
         if j >= 1:
             to_plane(j - 1)
-    tile = 512
-    slabs = ds // tile
     for j in range(nv):
         for i in range(slabs * j // nv, slabs * (j + 1) // nv):
-            ghead_ref[i * tile:(i + 1) * tile, :] = tn(hc_ref[:, i * tile:(i + 1) * tile], grad).astype(jnp.bfloat16)
+            ghead_ref[i * tile:(i + 1) * tile, :] = nn(hct[i * tile:(i + 1) * tile, :], grad).astype(jnp.bfloat16)
+        if j == 0:
+            for copy in waits:
+                copy.wait_send()
         total = mine[j, chip]
         for r in range(1, nc):
             remote(plane_in.at[j, r], plane_in.at[j, r], p_send.at[j, r], p_recv.at[j, r], {"dp": partner}).wait_recv()
             total = total + plane_in[j, r].astype(jnp.float32)
         if j < nv - 1:
             z_out[j] = total.astype(jnp.bfloat16)
-            go(remote(z_out.at[j], z_in.at[j], z_send.at[j], z_recv.at[j], {"vocab": lax.rem(vi + 1 + j, nv)}))
+            go(remote(z_out.at[j], z_in.at[j], z_send.at[j], z_recv.at[j], {"vocab": lax.rem(vi + 1 + j, nv)}), late)
         else:
             own[...] = total
     total = own[...]
@@ -307,7 +319,7 @@
         remote(z_in.at[j], z_in.at[j], z_send.at[j], z_recv.at[j], {"vocab": lax.rem(vi + 1, nv)}).wait_recv()
         total = total + z_in[j].astype(jnp.float32)
     gh_ref[...] = jnp.concatenate([total[:rows], total[rows:]], axis=1).astype(jnp.bfloat16)
-    for copy in waits:
+    for copy in late:
         copy.wait_send()
 
 
@@ -361,6 +373,7 @@
             pltpu.VMEM((2 * live, width), bf16),
             pltpu.VMEM((2 * live, width), bf16),
             pltpu.VMEM((live, ds), bf16),
+            pltpu.VMEM((ds, live), bf16),
             pltpu.VMEM((live, vocab), f32),
             pltpu.VMEM((live, vocab), f32),
             pltpu.VMEM((n, 8, lanes), f32),

time: 54.8 us -> 54.5 us (level)
  no operation moved by 1% of the time
where the time goes in v4:
time: 54.5 us; the launch traced here: 54.4 us
  Pallas kernels  48.3 us (89%)
  between operations  3.62 us (7%)
  local copies, waits for them, and re-layouts  2.46 us (5%)
    pallas_call x1, Pallas kernels, per_device(): pl.pallas_call(functools.partial(main_kernel, n, nv, rows, live, cuts, pi...  48.3 us
    unnamed x2, local copies, waits for them, and re-layouts  2.46 us

profile of v4, /device:TPU:0, one launch (start us, length us, event | category | flops | bytes accessed | tf_op | source)
XLA Modules:
  0.0 54.4 jit_solution(13889142274028821605)
XLA Ops:
  1.9 48.3 %distill.1 = (f32[1,1]{1,0:T(1,128)}, bf16[3584,512]{1,0:T(8,128)(2,1)S(1)}, bf16[24,896]{1,0:T(8,128)(2,1)S(1)}) custom-call(bf16[24,3584]{1,0:T(8,128)(2,1)} %sh_ref.1, bf16[24,4608]{1,0:T(8,128)(2,1)} %th_ref.1, s32[1]{0:T(128)S(6)} %copy.15.live_ref, s32[1]{0:T(128)S(6)} %copy.16.count_ref, s32[24]{0:T(128)} %dest_ref.1, bf16[3584,512]{1,0:T(8,128)(2,1)} %shead_hbm.1, ...), custom_call_target="tpu_custom_call" | custom-call | tf_op jit(solution)/shard_map/distill/pallas_call | solution.py:359
  50.2 0.6 %copy.13 = bf16[24,896]{1,0:T(8,128)(2,1)} copy(bf16[24,896]{1,0:T(8,128)(2,1)S(1)} %get-tuple-element.10) | data formatting | bytes 86016
  50.9 1.8 %copy.14 = bf16[3584,512]{1,0:T(8,128)(2,1)} copy(bf16[3584,512]{1,0:T(8,128)(2,1)S(1)} %get-tuple-element.11) | data formatting | bytes 7340032

commit v5 on v4

--- a/solution.py
+++ b/solution.py
@@ -49,7 +49,7 @@
     (
         gm, shead, thead, onehot_s, onehot_t, hc_ref, hct, s_log, t_log,
         st, sz, lgx, core_out, core_in, mine, plane_out, plane_in, own, z_out, z_in,
-        head_sem, m_send, m_recv, ici_send, core_send, g_recv, relay_send, relay_recv,
+        head_sem, m_send, m_recv, ici_send, core_send, g_recv, hop_send, hop_recv,
         st_send, st_recv, sz_send, sz_recv, c_send, c_recv, p_send, p_recv, z_send, z_recv,
     ) = scratch
     nc = n // 2
@@ -123,7 +123,9 @@
         copy.start()
         kept.append(copy)
 
-    square = nc == 4
+    square = nc == 4 and nv % 2 == 0
+    even = lax.rem(vi, 2)
+    z_pair = vi + 1 - 2 * even
     x_chip = 2 * lax.div(chip, 2) + 1 - lax.rem(chip, 2)
     y_chip = lax.rem(chip + 2, 4)
     targets = [x_chip, y_chip] if square else [lax.rem(chip + r, nc) for r in range(1, nc)]
@@ -132,29 +134,71 @@
     def block_copy(i, shard, send, target):
         return remote(bufs[i].at[shard], bufs[i].at[shard], send, g_recv.at[i, shard], {"dp": target})
 
+    def columns(i, shard, first, size):
+        return bufs[i].at[shard, :, pl.ds(pl.multiple_of(first * 128, 128), size * 128)]
+
+    def quarters(i):
+        units = bufs[i].shape[2] // 128
+        shared = units // 4
+        return (units - 2 * shared) // 2, shared
+
+    def hop(i, shard, first, size, slot, target):
+        part = columns(i, shard, first, size)
+        return remote(part, part, hop_send.at[i, slot], hop_recv.at[i, slot], target)
+
     def start_own(i):
-        for r, to in enumerate(targets):
-            go(block_copy(i, me, ici_send.at[i, r], 2 * to + core))
+        if square:
+            plain, shared = quarters(i)
+            for r, to in enumerate(targets):
+                target = {"dp": 2 * to + core}
+                go(hop(i, me, 0, 2 * plain, r, target))
+                go(hop(i, me, 2 * plain + even * shared, shared, 2 + r, target))
+        else:
+            for r, to in enumerate(targets):
+                go(block_copy(i, me, ici_send.at[i, r], 2 * to + core))
         go(block_copy(i, me, core_send.at[i, 0], partner))
 
     def pass_on(i):
         for r, source in enumerate(sources):
             shard = 2 * source + core
-            block_copy(i, shard, core_send.at[i, r + 1], partner).wait_recv()
             if square:
-                size = bufs[i].shape[2] // 2
-                to = (y_chip, x_chip)[r]
-                part = bufs[i].at[shard, :, pl.ds(r * size, size)]
-                go(remote(part, part, relay_send.at[i, r], relay_recv.at[i, r], {"dp": 2 * to + core}))
-            go(block_copy(i, shard, core_send.at[i, r + 1], partner))
+                plain, shared = quarters(i)
+                mate = {"dp": 2 * (y_chip, x_chip)[r] + core}
+                half_at = 2 * plain + even * shared
+                hop(i, shard, 0, 2 * plain, r, mate).wait_recv()
+                if r == 0:
+                    go(hop(i, shard, even * plain, plain, 6, mate))
+                hop(i, shard, half_at, shared, 2 + r, mate).wait_recv()
+                if r == 1:
+                    go(hop(i, shard, half_at, shared, 7, mate))
+                go(hop(i, shard, half_at, shared, 4 + r, {"vocab": z_pair}))
+            else:
+                block_copy(i, shard, core_send.at[i, r + 1], partner).wait_recv()
+                go(block_copy(i, shard, core_send.at[i, r + 1], partner))
+
+    def swap(i):
+        if square:
+            plain, shared = quarters(i)
+            mate = {"vocab": z_pair}
+            shard = 2 * (3 - chip) + core
+            odd = 1 - even
+            hop(i, shard, even * plain, plain, 6, mate).wait_recv()
+            go(hop(i, shard, even * plain, plain, 8, mate))
+            hop(i, shard, 2 * plain + even * shared, shared, 7, mate).wait_recv()
+            go(hop(i, shard, 2 * plain + even * shared, shared, 9, mate))
+            for r, source in enumerate(sources):
+                other = 2 * source + core
+                hop(i, other, 2 * plain + odd * shared, shared, 4 + r, mate).wait_recv()
+                go(block_copy(i, other, core_send.at[i, r + 1], partner))
 
     def finish(i):
         if square:
+            plain, shared = quarters(i)
+            mate = {"vocab": z_pair}
             shard = 2 * (3 - chip) + core
-            for r in range(2):
-                size = bufs[i].shape[2] // 2
-                part = bufs[i].at[shard, :, pl.ds(r * size, size)]
-                remote(part, part, relay_send.at[i, r], relay_recv.at[i, r], {"dp": partner}).wait_recv()
+            odd = 1 - even
+            hop(i, shard, odd * plain, plain, 8, mate).wait_recv()
+            hop(i, shard, 2 * plain + odd * shared, shared, 9, mate).wait_recv()
             go(block_copy(i, shard, core_send.at[i, 3], partner))
         for c in range(nc):
             block_copy(i, 2 * c + 1 - core, core_send.at[i, 0], partner).wait_recv()
@@ -200,17 +244,19 @@
         value = nn(top, head[at:at + size, :]) + nn(low, head[half + at:half + at + size, :])
         out[...] = value if at == 0 else out[...] + value
 
-    for i in range(npieces + 1):
+    for i in range(npieces + 2):
         if 0 < i < npieces:
             pass_on(i)
             if i + 2 < npieces:
                 start_own(i + 2)
-        if i >= 1:
-            finish(i - 1)
-            b, at, _ = cuts[i - 1]
+        if 1 <= i <= npieces:
+            swap(i - 1)
+        if i >= 2:
+            finish(i - 2)
+            b, at, _ = cuts[i - 2]
             if at == 0:
                 head_copies[b].wait()
-            logits(i - 1)
+            logits(i - 2)
 
     lanes = st.shape[2]
     s_val, t_val = s_log[...], t_log[...]
@@ -349,7 +395,7 @@
     dma = pltpu.SemaphoreType.DMA
     smem = pl.BlockSpec(memory_space=pltpu.SMEM)
     cuts = []
-    for b, sizes in enumerate(((1024, 768), (768, 768, 768))):
+    for b, sizes in enumerate(((1024, 768), (1024, 768, 512))):
         at = 0
         for size in sizes:
             cuts.append((b, at, size))
@@ -389,7 +435,7 @@
             pltpu.VMEM((nv, pair, half), bf16),
             dma((2,)),
             dma((n,)), dma((n,)),
-            dma((pieces, nc)), dma((pieces, nc)), dma((pieces, n)), dma((pieces, 2)), dma((pieces, 2)),
+            dma((pieces, nc)), dma((pieces, nc)), dma((pieces, n)), dma((pieces, 10)), dma((pieces, 10)),
             dma((n,)), dma((n,)), dma((nv,)), dma((nv,)),
             dma((nv,)), dma((nv,)), dma((nv, nc)), dma((nv, nc)), dma((nv,)), dma((nv,)),
         ],

time: 54.5 us -> 57 us (1.046)
  Pallas kernels: 48.3 us -> 50.7 us
    pallas_call x1, Pallas kernels: 48.3 us -> 50.7 us  [per_device(): pl.pallas_call(functools.partial(main_kernel, n, nv, rows, live, cuts, pi...]
where the time goes in v5:
time: 57 us; the launch traced here: 56.8 us
  Pallas kernels  50.7 us (89%)
  between operations  3.62 us (6%)
  local copies, waits for them, and re-layouts  2.46 us (4%)
    pallas_call x1, Pallas kernels, per_device(): pl.pallas_call(functools.partial(main_kernel, n, nv, rows, live, cuts, pi...  50.7 us
    unnamed x2, local copies, waits for them, and re-layouts  2.46 us

profile of v5, /device:TPU:0, one launch (start us, length us, event | category | flops | bytes accessed | tf_op | source)
XLA Modules:
  0.0 56.8 jit_solution(7252232702253719203)
XLA Ops:
  1.9 50.7 %distill.1 = (f32[1,1]{1,0:T(1,128)}, bf16[3584,512]{1,0:T(8,128)(2,1)S(1)}, bf16[24,896]{1,0:T(8,128)(2,1)S(1)}) custom-call(bf16[24,3584]{1,0:T(8,128)(2,1)} %sh_ref.1, bf16[24,4608]{1,0:T(8,128)(2,1)} %th_ref.1, s32[1]{0:T(128)S(6)} %copy.15.live_ref, s32[1]{0:T(128)S(6)} %copy.16.count_ref, s32[24]{0:T(128)} %dest_ref.1, bf16[3584,512]{1,0:T(8,128)(2,1)} %shead_hbm.1, ...), custom_call_target="tpu_custom_call" | custom-call | tf_op jit(solution)/shard_map/distill/pallas_call | solution.py:405
  52.7 0.6 %copy.13 = bf16[24,896]{1,0:T(8,128)(2,1)} copy(bf16[24,896]{1,0:T(8,128)(2,1)S(1)} %get-tuple-element.10) | data formatting | bytes 86016
  53.3 1.8 %copy.14 = bf16[3584,512]{1,0:T(8,128)(2,1)} copy(bf16[3584,512]{1,0:T(8,128)(2,1)S(1)} %get-tuple-element.11) | data formatting | bytes 7340032

commit v6 on v4

--- a/solution.py
+++ b/solution.py
@@ -349,7 +349,7 @@
     dma = pltpu.SemaphoreType.DMA
     smem = pl.BlockSpec(memory_space=pltpu.SMEM)
     cuts = []
-    for b, sizes in enumerate(((1024, 768), (768, 768, 768))):
+    for b, sizes in enumerate(((1792,), (1280, 1024))):
         at = 0
         for size in sizes:
             cuts.append((b, at, size))

time: 54.5 us -> 53.4 us (0.980)
  Pallas kernels: 48.3 us -> 47.1 us
    pallas_call x1, Pallas kernels: 48.3 us -> 47.1 us  [per_device(): pl.pallas_call(functools.partial(main_kernel, n, nv, rows, live, cuts, pi...]
where the time goes in v6:
time: 53.4 us; the launch traced here: 53.2 us
  Pallas kernels  47.1 us (88%)
  between operations  3.62 us (7%)
  local copies, waits for them, and re-layouts  2.46 us (5%)
    pallas_call x1, Pallas kernels, per_device(): pl.pallas_call(functools.partial(main_kernel, n, nv, rows, live, cuts, pi...  47.1 us
    unnamed x2, local copies, waits for them, and re-layouts  2.46 us

profile of v6, /device:TPU:0, one launch (start us, length us, event | category | flops | bytes accessed | tf_op | source)
XLA Modules:
  0.0 53.2 jit_solution(10819161696840516369)
XLA Ops:
  1.9 47.1 %distill.1 = (f32[1,1]{1,0:T(1,128)}, bf16[3584,512]{1,0:T(8,128)(2,1)S(1)}, bf16[24,896]{1,0:T(8,128)(2,1)S(1)}) custom-call(bf16[24,3584]{1,0:T(8,128)(2,1)} %sh_ref.1, bf16[24,4608]{1,0:T(8,128)(2,1)} %th_ref.1, s32[1]{0:T(128)S(6)} %copy.15.live_ref, s32[1]{0:T(128)S(6)} %copy.16.count_ref, s32[24]{0:T(128)} %dest_ref.1, bf16[3584,512]{1,0:T(8,128)(2,1)} %shead_hbm.1, ...), custom_call_target="tpu_custom_call" | custom-call | tf_op jit(solution)/shard_map/distill/pallas_call | solution.py:359
  49.1 0.6 %copy.13 = bf16[24,896]{1,0:T(8,128)(2,1)} copy(bf16[24,896]{1,0:T(8,128)(2,1)S(1)} %get-tuple-element.10) | data formatting | bytes 86016
  49.7 1.8 %copy.14 = bf16[3584,512]{1,0:T(8,128)(2,1)} copy(bf16[3584,512]{1,0:T(8,128)(2,1)S(1)} %get-tuple-element.11) | data formatting | bytes 7340032

commit v7 on v6

--- a/solution.py
+++ b/solution.py
@@ -282,23 +282,36 @@
         ]
         for c in range(nc):
             core_out[j, c] = blocks[c].astype(jnp.bfloat16)
-        go(remote(core_out.at[j], core_in.at[j], c_send.at[j], c_recv.at[j], {"dp": partner}))
         for c in range(nc):
             mine[j, c] = blocks[nc + c]
 
-    def to_plane(j):
-        remote(core_out.at[j], core_in.at[j], c_send.at[j], c_recv.at[j], {"dp": partner}).wait_recv()
-        mine[j] = mine[j] + core_in[j].astype(jnp.float32)
-        plane_out[j] = mine[j].astype(jnp.bfloat16)
+    group = nv // 2 if nv % 2 == 0 else nv
+
+    def cross_core(first):
+        at = pl.ds(first, group)
+        return remote(core_out.at[at], core_in.at[at], c_send.at[first], c_recv.at[first], {"dp": partner})
+
+    def plane(first, r, to):
+        at = pl.ds(first, group)
+        return remote(
+            plane_out.at[at, to], plane_in.at[at, r], p_send.at[first, r], p_recv.at[first, r], {"dp": 2 * to + core}
+        )
+
+    def to_plane(first):
+        cross_core(first).wait_recv()
+        at = pl.ds(first, group)
+        mine[at] = mine[at] + core_in[at].astype(jnp.float32)
+        plane_out[at] = mine[at].astype(jnp.bfloat16)
         for r in range(1, nc):
-            to = lax.rem(chip + r, nc)
-            go(remote(plane_out.at[j, to], plane_in.at[j, r], p_send.at[j, r], p_recv.at[j, r], {"dp": 2 * to + core}), late)
-
-    for j in range(nv + 1):
-        if j < nv:
-            partial(j)
-        if j >= 1:
-            to_plane(j - 1)
+            go(plane(first, r, lax.rem(chip + r, nc)), late)
+
+    for first in range(0, nv + group, group):
+        if first < nv:
+            for j in range(first, first + group):
+                partial(j)
+            go(cross_core(first))
+        if first >= group:
+            to_plane(first - group)
     for j in range(nv):
         for i in range(slabs * j // nv, slabs * (j + 1) // nv):
             ghead_ref[i * tile:(i + 1) * tile, :] = nn(hct[i * tile:(i + 1) * tile, :], grad).astype(jnp.bfloat16)
@@ -307,7 +320,8 @@
                 copy.wait_send()
         total = mine[j, chip]
         for r in range(1, nc):
-            remote(plane_in.at[j, r], plane_in.at[j, r], p_send.at[j, r], p_recv.at[j, r], {"dp": partner}).wait_recv()
+            if j % group == 0:
+                plane(j, r, lax.rem(chip + r, nc)).wait_recv()
             total = total + plane_in[j, r].astype(jnp.float32)
         if j < nv - 1:
             z_out[j] = total.astype(jnp.bfloat16)

time: 53.4 us -> 56.1 us (1.051)
  Pallas kernels: 47.1 us -> 49.8 us
    pallas_call x1, Pallas kernels: 47.1 us -> 49.8 us  [per_device(): pl.pallas_call(functools.partial(main_kernel, n, nv, rows, live, cuts, pi...]
where the time goes in v7:
time: 56.1 us; the launch traced here: 55.9 us
  Pallas kernels  49.8 us (89%)
  between operations  3.62 us (6%)
  local copies, waits for them, and re-layouts  2.46 us (4%)
    pallas_call x1, Pallas kernels, per_device(): pl.pallas_call(functools.partial(main_kernel, n, nv, rows, live, cuts, pi...  49.8 us
    unnamed x2, local copies, waits for them, and re-layouts  2.46 us

profile of v7, /device:TPU:0, one launch (start us, length us, event | category | flops | bytes accessed | tf_op | source)
XLA Modules:
  0.0 55.9 jit_solution(781519388526393318)
XLA Ops:
  1.9 49.8 %distill.1 = (f32[1,1]{1,0:T(1,128)}, bf16[3584,512]{1,0:T(8,128)(2,1)S(1)}, bf16[24,896]{1,0:T(8,128)(2,1)S(1)}) custom-call(bf16[24,3584]{1,0:T(8,128)(2,1)} %sh_ref.1, bf16[24,4608]{1,0:T(8,128)(2,1)} %th_ref.1, s32[1]{0:T(128)S(6)} %copy.15.live_ref, s32[1]{0:T(128)S(6)} %copy.16.count_ref, s32[24]{0:T(128)} %dest_ref.1, bf16[3584,512]{1,0:T(8,128)(2,1)} %shead_hbm.1, ...), custom_call_target="tpu_custom_call" | custom-call | tf_op jit(solution)/shard_map/distill/pallas_call | solution.py:373
  51.8 0.6 %copy.13 = bf16[24,896]{1,0:T(8,128)(2,1)} copy(bf16[24,896]{1,0:T(8,128)(2,1)S(1)} %get-tuple-element.10) | data formatting | bytes 86016
  52.4 1.8 %copy.14 = bf16[3584,512]{1,0:T(8,128)(2,1)} copy(bf16[3584,512]{1,0:T(8,128)(2,1)S(1)} %get-tuple-element.11) | data formatting | bytes 7340032
